TPU v7x, 128 devices: a whole 4x4x4 slice. The times are simulated.
128 devices in a mesh: row: 8 (over x, z_hi), col: 8 (over y, z_lo), dp: 2 (over core).
Axes of the slice: x: 4, y: 4, z: 4 (z_hi: 2, z_lo: 2; z = z_hi * 2 + z_lo), core: 2. Of those that a mesh axis runs over, the one named last changes fastest.
Arguments:
- hid_query: bfloat16 [16384, 4096], P(('row', 'col', 'dp')), may hold values from -6 to 6
- hid_key: bfloat16 [16384, 4096], P(('row', 'col', 'dp')), may hold values from -6 to 6
- projection: bfloat16 [4096, 1024], replicated, may hold values from -0.09375 to 0.09375
- tile_rows: int32 [8, 8, 48], P('row', 'col'), may hold values from 0 to 7, as said below
- tile_cols: int32 [8, 8, 48], P('row', 'col'), may hold values from 0 to 7, as said below
- tile_count: int32 [8, 8], P('row', 'col'), may hold values from 1 to 48, as said below
- positive: int32 [16384], P(('row', 'col', 'dp')), may hold values from 0 to 16383, as said below
Outputs:
- grad_projection: float32 [4096, 1024], P(('row', 'col', 'dp'))
Inputs may be any that keep to these rules, and one draw needn't show every extreme that they name: Entry s of cell (r, c) names tile (tile_rows, tile_cols); the 48 entries of one cell name distinct tiles. `tile_cols`: see tile_rows. `tile_count`: some cell of every draw uses all 48 entries. `positive`: maps each device's 128 documents one to one onto the same device's documents.
All inputs are finite; a program needn't handle non-finite values.
Results may differ from a plain program's by a relative error of at most 0.0095.
Values may be sent and summed in bfloat16 or wider, within the bound.
No kernel may reach another device: no remote copies, remote signals or barrier semaphores. Data moves between devices by JAX's collectives and lax.ppermute only.
A program may use at most 128 MiB of HBM per device.

v0:
```python
import jax
import jax.numpy as jnp
from jax import lax
from jax.sharding import PartitionSpec as P

TILE = 256


TAU_INV = 20.0
EPS = 1e-06


def unit_rows(raw):
    values = raw.astype(jnp.float32)
    scale = lax.rsqrt(jnp.sum(values * values, axis=1, keepdims=True) + EPS)
    return (values * scale, scale)


def contract_docs(left, right):
    return lax.dot_general(
        left, right, (((0,), (0,)), ((), ())), preferred_element_type=jnp.float32
    )


def add_block(total, addend, start):
    start = jnp.asarray(start)
    shape = (addend.shape[0],) + total.shape[1:]
    zeros = (jnp.zeros((), jnp.int32),) * (total.ndim - 1)
    old = lax.dynamic_slice(total, (start,) + zeros, shape)
    return lax.dynamic_update_slice(total, old + addend, (start,) + zeros)


def local(hid_query, hid_key, projection, tile_rows, tile_cols, tile_count, positive):
    doc_rows = hid_query.shape[0]
    embed = projection.shape[1]
    col_size = lax.axis_size("col")
    core_size = lax.axis_size("dp")
    row_index = lax.axis_index("row")
    col_index = lax.axis_index("col")
    core_index = lax.axis_index("dp")
    query_raw = jnp.dot(hid_query, projection, preferred_element_type=jnp.float32).astype(
        jnp.bfloat16
    )
    key_raw = jnp.dot(hid_key, projection, preferred_element_type=jnp.float32).astype(jnp.bfloat16)
    query_exact, query_scale = unit_rows(query_raw)
    key_exact, key_scale = unit_rows(key_raw)
    query_unit = query_exact.astype(jnp.bfloat16)
    key_unit = key_exact.astype(jnp.bfloat16)
    owner_block = (row_index * col_size + col_index) * core_size + core_index
    local_pos = positive - owner_block * doc_rows
    paired = key_unit[local_pos]
    pos_score = (
        jnp.sum(query_unit.astype(jnp.float32) * paired.astype(jnp.float32), axis=1) * TAU_INV
    )
    pos_exp = jnp.exp(pos_score)
    key_pos_exp = jnp.zeros((doc_rows,), jnp.float32).at[local_pos].add(pos_exp)
    query_block = lax.all_gather(query_unit, ("col", "dp"), axis=0, tiled=True)
    key_block = lax.all_gather(key_unit, ("row", "dp"), axis=0, tiled=True)
    query_span = query_block.shape[0]
    key_span = key_block.shape[0]
    own_query = (col_index * core_size + core_index) * doc_rows
    own_key = (row_index * core_size + core_index) * doc_rows
    cell_rows = tile_rows[0, 0]
    cell_cols = tile_cols[0, 0]
    cell_count = tile_count[0, 0]
    entries = cell_rows.shape[0]
    share = entries // core_size
    first_entry = core_index * share
    my_tiles = jnp.clip(cell_count - first_entry, 0, share)
    stride = 1

    def tile_at(number):
        entry = first_entry + number * stride
        row_start = cell_rows[entry] * TILE
        col_start = cell_cols[entry] * TILE
        query_tile = lax.dynamic_slice_in_dim(query_block, row_start, TILE, 0)
        key_tile = lax.dynamic_slice_in_dim(key_block, col_start, TILE, 0)
        score = jnp.dot(query_tile, key_tile.T, preferred_element_type=jnp.float32) * TAU_INV
        return (row_start, col_start, query_tile, key_tile, score)

    def first_pass(number, sums):
        row_sum, col_sum = sums
        row_start, col_start, _, _, score = tile_at(number)
        expo = jnp.exp(score)
        row_sum = add_block(row_sum, jnp.sum(expo, axis=1), row_start)
        col_sum = add_block(col_sum, jnp.sum(expo, axis=0), col_start)
        return (row_sum, col_sum)

    row_sum = add_block(jnp.zeros((query_span,), jnp.float32), pos_exp, own_query)
    col_sum = add_block(jnp.zeros((key_span,), jnp.float32), key_pos_exp, own_key)
    row_sum, col_sum = lax.fori_loop(0, my_tiles, first_pass, (row_sum, col_sum))
    row_log = jnp.log(lax.psum(row_sum, ("col", "dp")))
    col_log = jnp.log(lax.psum(col_sum, ("row", "dp")))

    def second_pass(number, grads):
        query_acc, key_acc = grads
        row_start, col_start, query_tile, key_tile, score = tile_at(number)
        row_part = lax.dynamic_slice_in_dim(row_log, row_start, TILE, 0)
        col_part = lax.dynamic_slice_in_dim(col_log, col_start, TILE, 0)
        weight = (jnp.exp(score - row_part[:, None]) + jnp.exp(score - col_part[None, :])).astype(
            jnp.bfloat16
        )
        query_add = jnp.dot(weight, key_tile, preferred_element_type=jnp.float32) * TAU_INV
        key_add = contract_docs(weight, query_tile) * TAU_INV
        return (add_block(query_acc, query_add, row_start), add_block(key_acc, key_add, col_start))

    query_acc, key_acc = lax.fori_loop(
        0,
        my_tiles,
        second_pass,
        (jnp.zeros((query_span, embed), jnp.float32), jnp.zeros((key_span, embed), jnp.float32)),
    )
    query_grad = lax.psum_scatter(query_acc, ("col", "dp"), scatter_dimension=0, tiled=True)
    key_grad = lax.psum_scatter(key_acc, ("row", "dp"), scatter_dimension=0, tiled=True)
    row_own = lax.dynamic_slice_in_dim(row_log, own_query, doc_rows, 0)
    col_own = lax.dynamic_slice_in_dim(col_log, own_key, doc_rows, 0)
    pos_weight = jnp.exp(pos_score - row_own) + jnp.exp(pos_score - col_own[local_pos]) - 2.0
    query_grad = query_grad + pos_weight[:, None] * paired.astype(jnp.float32) * TAU_INV
    key_grad = key_grad + jnp.zeros((doc_rows, embed), jnp.float32).at[local_pos].add(
        pos_weight[:, None] * query_unit.astype(jnp.float32) * TAU_INV
    )
    query_back = (
        query_scale
        * (query_grad - query_exact * jnp.sum(query_exact * query_grad, axis=1, keepdims=True))
    ).astype(jnp.bfloat16)
    key_back = (
        key_scale * (key_grad - key_exact * jnp.sum(key_exact * key_grad, axis=1, keepdims=True))
    ).astype(jnp.bfloat16)
    return lax.psum_scatter(
        contract_docs(hid_query, query_back) + contract_docs(hid_key, key_back),
        ("row", "col", "dp"),
        scatter_dimension=0,
        tiled=True,
    )


def solution(mesh):
    return jax.shard_map(
        local,
        mesh=mesh,
        in_specs=(
            P(("row", "col", "dp"), None),
            P(("row", "col", "dp"), None),
            P(),
            P("row", "col", None),
            P("row", "col", None),
            P("row", "col"),
            P(("row", "col", "dp")),
        ),
        out_specs=P(("row", "col", "dp"), None),
        check_vma=False,
    )
```

profile of v0, /device:TPU:0, one launch (start us, length us, event | category | flops | bytes accessed | tf_op | source)
XLA Modules:
  0.0 1414.3 jit_solution(6197500479472638574)
XLA Ops:
  6.5 5.1 multiply_reduce_fusion.2
  14.7 4.7 multiply_reduce_fusion.3
  22.9 48.4 %all-gather.5.cloned.1.call-done = bf16[2048,1024]{1,0:T(8,128)(2,1)} async-done(((bf16[128,1024]{1,0:T(8,128)(2,1)}), bf16[2048,1024]{1,0:T(8,128)(2,1)}) %all-gather.5.cloned.1.call-update) | async-done | bytes 4194320 | tf_op jit(solution)/shard_map/all_gather | solution.py:58
  71.3 37.8 %all-gather.3.cloned.1.call-done = bf16[2048,1024]{1,0:T(8,128)(2,1)} async-done(((bf16[128,1024]{1,0:T(8,128)(2,1)}), bf16[2048,1024]{1,0:T(8,128)(2,1)}) %all-gather.3.cloned.1.call-update) | async-done | bytes 4194320 | tf_op jit(solution)/shard_map/all_gather | solution.py:57
  109.0 110.5 %while.24 = (s32[]{:T(128)}, f32[2048]{0:T(1024)S(1)}, f32[2048]{0:T(1024)S(1)}, s32[]{:T(128)}, s32[]{:T(128)}, /*index=5*/s32[48]{0:T(128)S(1)}, bf16[2048,102...) while((s32[]{:T(128)}, f32[2048]{0:T(1024)S(1)}, ...), condition=%wide.region_7.8_spmd, body=%wide.region_4.7_spmd.sunk | while | flops 134414352 | bytes 1057087 | solution.py:91
  219.5 33.7 %psum.15 = f32[2048]{0:T(1024)S(1)} all-reduce(f32[2048]{0:T(1024)S(1)} %get-tuple-element.114), channel_id=1, replica_groups=mesh['row'=8,'col'=8,'dp'=2] {'row','dp'}, use_global_device_ids=true, to_apply=%region_9.10 | all-reduce | flops 2048 | bytes 16384 | tf_op jit(solution)/shard_map/psum | solution.py:93
  253.2 28.2 %psum.14 = f32[2048]{0:T(1024)S(1)} all-reduce(f32[2048]{0:T(1024)S(1)} %get-tuple-element.113), channel_id=1, replica_groups=mesh['row'=8,'col'=8,'dp'=2] {'col','dp'}, use_global_device_ids=true, to_apply=%region_8.9 | all-reduce | flops 2048 | bytes 16384 | tf_op jit(solution)/shard_map/psum | solution.py:92
  281.5 4.3 broadcast.46.clone
  285.8 4.3 broadcast.46
  290.1 225.5 %while.25 = (s32[]{:T(128)}, f32[2048,1024]{1,0:T(8,128)}, f32[2048,1024]{1,0:T(8,128)}, s32[]{:T(128)}, s32[]{:T(128)}, /*index=5*/s32[48]{0:T(128)S(1)}, bf16[...) while((s32[]{:T(128)}, f32[2048,1024]{1,0:T(8,128)}, ...), condition=%wide.region_11.12_spmd, body=%wide.region_10.11_spmd.sunk | while | flops 404029440 | bytes 6691167 | solution.py:107
  303.4 2.8 fusion.66
  322.2 2.8 fusion.66
  341.1 2.7 fusion.66
  362.5 2.7 fusion.65
  369.3 2.7 fusion.66
  378.7 2.7 fusion.66
  397.4 2.7 fusion.66
  406.8 2.7 fusion.66
  409.5 2.7 fusion.65
  428.3 2.7 fusion.65
  453.8 2.8 fusion.66
  456.5 2.7 fusion.65
  475.3 2.7 fusion.65
  491.4 2.7 fusion.66
  500.8 2.7 fusion.66
  517.6 95.3 %reduce-scatter.8.cloned.1.call-done = f32[128,1024]{1,0:T(8,128)} async-done(((f32[2048,1024]{1,0:T(8,128)}), f32[128,1024]{1,0:T(8,128)}) %reduce-scatter.8.cloned.1.call-update) | async-done | bytes 524304 | tf_op jit(solution)/shard_map/reduce_scatter | solution.py:114
  612.9 3.5 scatter_custom_fusion.1
  617.7 91.3 %reduce-scatter.6.cloned.1.call-done = f32[128,1024]{1,0:T(8,128)} async-done(((f32[2048,1024]{1,0:T(8,128)}), f32[128,1024]{1,0:T(8,128)}) %reduce-scatter.6.cloned.1.call-update) | async-done | bytes 524304 | tf_op jit(solution)/shard_map/reduce_scatter | solution.py:113
  710.3 3.7 fusion.27
  714.0 8.2 add_bitcast_fusion
  722.3 17.5 %copy.11 = f32[4096,1024]{1,0:T(8,128)} copy(f32[4096,1024]{0,1:T(8,128)} %add_bitcast_fusion) | data formatting | bytes 33554432
  739.8 668.0 %reduce-scatter.10.cloned.1.call-done = f32[32,1024]{1,0:T(8,128)} async-done(((f32[4096,1024]{1,0:T(8,128)}), f32[32,1024]{1,0:T(8,128)}) %reduce-scatter.10.cloned.1.call-update) | async-done | bytes 131088 | tf_op jit(solution)/shard_map/reduce_scatter | solution.py:129
  (294 shorter events, 243.6 us)
Async XLA Ops:
  6.5 8.1 copy-start
  6.5 6.0 copy-start.5
  6.5 64.7 %all-gather.5.cloned.1.call-start = ((), (), s32[]{:S(2)}) async-start(), calls=%async_computation.4 | async-start | bytes 4456448 | tf_op jit(solution)/shard_map/all_gather | solution.py:58
  12.5 96.5 %all-gather.3.cloned.1.call-start = ((), (), s32[]{:S(2)}) async-start(), calls=%async_computation.3 | async-start | bytes 4456448 | tf_op jit(solution)/shard_map/all_gather | solution.py:57
  14.6 94.4 %copy-start.6 = (s32[1,1,48]{2,1,0:T(1,128)S(1)}, s32[1,1,48]{2,1,0:T(1,128)}, u32[]{:S(2)}) copy-start(s32[1,1,48]{2,1,0:T(1,128)} %param.14) | copy-start | bytes 580
  14.7 94.4 %copy-start.7 = (s32[1,1,48]{2,1,0:T(1,128)S(1)}, s32[1,1,48]{2,1,0:T(1,128)}, u32[]{:S(2)}) copy-start(s32[1,1,48]{2,1,0:T(1,128)} %param.15) | copy-start | bytes 580
  20.3 592.6 %reduce-scatter.8.cloned.1.call-start = ((), (), s32[]{:S(2)}) async-start(), calls=%async_computation.6 | async-start | bytes 8912896 | tf_op jit(solution)/shard_map/reduce_scatter | solution.py:114
  515.5 97.4 %copy-start.4 = (bf16[128,1024]{1,0:T(8,128)(2,1)S(1)}, bf16[128,1024]{1,0:T(8,128)(2,1)}, u32[]{:S(2)}) copy-start(bf16[128,1024]{1,0:T(8,128)(2,1)} %get-tuple-element.160) | copy-start | bytes 786436
  515.6 193.4 %reduce-scatter.6.cloned.1.call-start = ((), (), s32[]{:S(2)}) async-start(), calls=%async_computation.5 | async-start | bytes 8912896 | tf_op jit(solution)/shard_map/reduce_scatter | solution.py:113
  516.2 891.6 %reduce-scatter.10.cloned.1.call-start = ((), (), s32[]{:S(2)}) async-start(), calls=%async_computation.7 | async-start | bytes 16908288 | tf_op jit(solution)/shard_map/reduce_scatter | solution.py:129
  710.3 3.7 copy-start.2
  710.3 3.7 copy-start.3
  739.7 668.0 %copy-start.1 = (bf16[128,4096]{1,0:T(8,128)(2,1)S(1)}, bf16[128,4096]{1,0:T(8,128)(2,1)}, u32[]{:S(2)}) copy-start(bf16[128,4096]{1,0:T(8,128)(2,1)} %param.11) | copy-start | bytes 3145732
Sparse Core Ops, SparseCore 0:
  12.6 58.5 all-gather.4
  73.0 36.0 all-gather.2
  515.7 97.1 reduce-scatter.7
  615.2 93.7 reduce-scatter.5
  739.9 667.8 reduce-scatter.9
where the time goes:
time: 1420 us; the launch traced here: 1410 us
  waiting for transfers between devices  941 us (66%)
  matrix products  228 us (16%)
  local copies, waits for them, and re-layouts  92.2 us (6%)
  blocking collectives  61.9 us (4%)
  loops' own time  61.8 us (4%)
  other arithmetic  14.7 us (1%)
    reduce_scatter x1, waiting for transfers between devices, local(): lax.psum_scatter(contract_docs(hid_query, query_back) + contract_docs(hid...  668 us
    reduce_scatter x1, waiting for transfers between devices, local(): lax.psum_scatter(key_acc, ('row', 'dp'), scatter_dimension=0, tiled=True)  95.3 us
    reduce_scatter x1, waiting for transfers between devices, local(): lax.psum_scatter(query_acc, ('col', 'dp'), scatter_dimension=0, tiled=True)  91.3 us
    dot_general x26, matrix products, contract_docs(): lax.dot_general(left, right, (((0,), (0,)), ((), ())), preferred_element_...  76.9 us
    dot_general x48, matrix products, tile_at(): jnp.dot(query_tile, key_tile.T, preferred_element_type=jnp.float32)  76.8 us
    dot_general x24, matrix products, second_pass(): jnp.dot(weight, key_tile, preferred_element_type=jnp.float32) * TAU_INV  64.4 us
    all_gather x1, waiting for transfers between devices, local(): key_block = lax.all_gather(key_unit, ('row', 'dp'), axis=0, tiled=True)  48.4 us
    all_gather x1, waiting for transfers between devices, local(): query_block = lax.all_gather(query_unit, ('col', 'dp'), axis=0, tiled=True)  37.8 us
  transfers between devices with their start and end apart: 5, of which 5 were waited for; matrix products, arithmetic and copies ran while one was open for 1% of the time, Pallas kernels for 0%

commit v1 on v0

v1 whole, which is shorter than its diff:
```python
import jax
import jax.numpy as jnp
from jax import lax
from jax.experimental import pallas as pl
from jax.experimental.pallas import tpu as pltpu
from jax.sharding import PartitionSpec as P

TAU_INV = 20.0
EPS = 1e-06
LOG2E = 1.4426950408889634
DOCS = 128
EMB = 1024
HID = 4096
BF = jnp.bfloat16
F32 = jnp.float32
VM = 56 * 1024 * 1024


def ring_pair(step, flip):
    return [(i, ((i // 2 + step) % 4) * 2 + ((i % 2) ^ flip)) for i in range(8)]


def move_query(value, step, flip):
    return lax.ppermute(value, "col", ring_pair(step, flip))


def move_key(value, step, flip):
    return lax.ppermute(value, "row", ring_pair(step, flip))


def move_z(value, step):
    pairs = []
    for r in range(8):
        for c in range(8):
            z = ((r % 2) * 2 + c % 2 + step) % 4
            pairs.append((r * 8 + c, ((r // 2) * 2 + z // 2) * 8 + (c // 2) * 2 + z % 2))
    return lax.ppermute(value, ("row", "col"), pairs)


def chip(x, y, z):
    return (x * 2 + z // 2) * 8 + y * 2 + z % 2


Z_GROUPS = [
    [chip(x, y, z) * 2 + core for z in range(4) for core in range(2)]
    for x in range(4)
    for y in range(4)
]
XY_GROUPS = [[chip(x, y, z) for x in range(4) for y in range(4)] for z in range(4)]


def swap(value):
    return lax.ppermute(value, "dp", [(0, 1), (1, 0)])


def params():
    return pltpu.CompilerParams(vmem_limit_bytes=VM)


def sds(shape, dtype):
    return jax.ShapeDtypeStruct(shape, dtype)


ANY = pl.BlockSpec(memory_space=pl.ANY)
SMEM = pl.BlockSpec(memory_space=pltpu.SMEM)
VMEM = pl.BlockSpec(memory_space=pltpu.VMEM)


def dot(a, b):
    return lax.dot_general(a, b, (((1,), (0,)), ((), ())), preferred_element_type=F32)


def dot_t(a, b):
    return lax.dot_general(a, b, (((1,), (1,)), ((), ())), preferred_element_type=F32)


def t_dot(a, b):
    return lax.dot_general(a, b, (((0,), (0,)), ((), ())), preferred_element_type=F32)


def unit_of(raw):
    values = raw.astype(F32)
    scale = lax.rsqrt(jnp.sum(values * values, axis=1, keepdims=True) + EPS)
    return values * scale, scale


def project_body(hq, hk, proj, q_unit, k_unit, q_raw, k_raw, hid, acc):
    step = pl.program_id(0)
    hid[:DOCS, :] = hq[...]
    hid[DOCS:, :] = hk[...]
    part = dot(hid[...], proj[...])

    @pl.when(step == 0)
    def _():
        acc[...] = part

    @pl.when(step > 0)
    def _():
        acc[...] += part

    @pl.when(step == pl.num_programs(0) - 1)
    def _():
        for raw_ref, unit_ref, start in ((q_raw, q_unit, 0), (k_raw, k_unit, DOCS)):
            raw = acc[start : start + DOCS, :].astype(BF)
            raw_ref[...] = raw
            unit_ref[...] = unit_of(raw)[0].astype(BF)


def project(hid_query, hid_key, projection):
    depth = 1024
    whole = pl.BlockSpec((DOCS, EMB), lambda i: (0, 0))
    return pl.pallas_call(
        project_body,
        grid=(HID // depth,),
        in_specs=[
            pl.BlockSpec((DOCS, depth), lambda i: (0, i)),
            pl.BlockSpec((DOCS, depth), lambda i: (0, i)),
            pl.BlockSpec((depth, EMB), lambda i: (i, 0)),
        ],
        out_specs=[whole] * 4,
        out_shape=[sds((DOCS, EMB), BF)] * 4,
        scratch_shapes=[pltpu.VMEM((2 * DOCS, depth), BF), pltpu.VMEM((2 * DOCS, EMB), F32)],
        compiler_params=params(),
    )(hid_query, hid_key, projection)


def one_hot(pos):
    lane = lax.broadcasted_iota(jnp.int32, (DOCS, DOCS), 1)
    return (lane == pos).astype(F32)


def eye():
    lane = lax.broadcasted_iota(jnp.int32, (DOCS, DOCS), 1)
    row = lax.broadcasted_iota(jnp.int32, (DOCS, DOCS), 0)
    return (lane == row).astype(F32)


def pairs_body(q_unit, k_unit, pos, paired, q_perm, pos_rows):
    hot = one_hot(pos[...])
    hot_bf = hot.astype(BF)
    pair = dot(hot_bf, k_unit[...])
    paired[...] = pair.astype(BF)
    q_perm[...] = t_dot(hot_bf, q_unit[...]).astype(BF)
    score = jnp.sum(q_unit[...].astype(F32) * pair, axis=1, keepdims=True) * TAU_INV
    expo = jnp.exp(score)
    pos_rows[0:1, :] = jnp.sum(eye() * expo, axis=0, keepdims=True)
    pos_rows[1:2, :] = jnp.sum(hot * expo, axis=0, keepdims=True)
    pos_rows[2:8, :] = jnp.zeros((6, DOCS), F32)


def pair_up(q_unit, k_unit, pos):
    return pl.pallas_call(
        pairs_body,
        in_specs=[VMEM] * 3,
        out_specs=[VMEM] * 3,
        out_shape=[sds((DOCS, EMB), BF), sds((DOCS, EMB), BF), sds((8, DOCS), F32)],
        compiler_params=params(),
    )(q_unit, k_unit, pos)


def scores_body(*refs):
    q_in, k_in = refs[0:4], refs[4:12]
    mask, pos_rows = refs[12:14]
    e_own, e_oth, sums = refs[14:17]
    q_s, k_s, e_s, acc, in_sems, out_sems = refs[17:23]
    loads = [
        pltpu.make_async_copy(ref, q_s.at[pl.ds(s * 256, 256)], in_sems.at[s])
        for s, ref in enumerate(q_in)
    ] + [
        pltpu.make_async_copy(ref, k_s.at[pl.ds(s * 256, 256)], in_sems.at[4 + s])
        for s, ref in enumerate(k_in)
    ]
    order = [4, 0, 1, 2, 3] + list(range(5, 12))
    for i in order:
        loads[i].start()
    stores = []
    for b in range(8):
        loads[4 + b].wait()
        total = [None, None]
        for m in range(4):
            if b == 0:
                loads[m].wait()
            chunk = slice(m * 256, (m + 1) * 256)
            score = dot_t(q_s[chunk, :], k_s[b * 256 : (b + 1) * 256, :])
            for n in range(2):
                a = m * 2 + n
                rows = slice(a * DOCS, (a + 1) * DOCS)
                expo = jnp.exp2(score[n * DOCS : (n + 1) * DOCS, :] * (TAU_INV * LOG2E))
                both = None
                for half in range(2):
                    slot = (b % 4) * 2 + half
                    one = expo[:, half * DOCS : (half + 1) * DOCS] * mask[a, slot]
                    e_s[b, rows, half * DOCS : (half + 1) * DOCS] = one.astype(BF)
                    both = one if half == 0 else both + one
                    part = one.reshape(16, 8, DOCS).sum(axis=0)
                    total[half] = part if a == 0 else total[half] + part
                if b == 0:
                    acc[rows, :] = both
                else:
                    acc[rows, :] += both
        out = (e_own if b < 4 else e_oth).at[:, pl.ds((b % 4) * 256, 256)]
        stores.append(pltpu.make_async_copy(e_s.at[b], out, out_sems.at[b]))
        stores[-1].start()
        for half in range(2):
            col = jnp.sum(total[half], axis=0, keepdims=True)
            if b == 0 and half == 0:
                col = col + pos_rows[1:2, :]
            sums[8 + 2 * b + half : 9 + 2 * b + half, :] = col
    for a in range(8):
        part = jnp.sum(acc[a * DOCS : (a + 1) * DOCS, :].T, axis=0, keepdims=True)
        if a == 0:
            part = part + pos_rows[0:1, :]
        sums[a : a + 1, :] = part
    for store in stores:
        store.wait()


def scores(q_in, k_in, mask, pos_rows):
    return pl.pallas_call(
        scores_body,
        in_specs=[ANY] * 12 + [SMEM, VMEM],
        out_specs=[ANY, ANY, VMEM],
        out_shape=[
            sds((8 * DOCS, 8 * DOCS), BF),
            sds((8 * DOCS, 8 * DOCS), BF),
            sds((24, DOCS), F32),
        ],
        scratch_shapes=[
            pltpu.VMEM((8 * DOCS, EMB), BF),
            pltpu.VMEM((16 * DOCS, EMB), BF),
            pltpu.VMEM((8, 8 * DOCS, 256), BF),
            pltpu.VMEM((8 * DOCS, DOCS), F32),
            pltpu.SemaphoreType.DMA((12,)),
            pltpu.SemaphoreType.DMA((8,)),
        ],
        compiler_params=params(),
    )(*q_in, *k_in, mask, pos_rows)


def grads_body(*refs):
    q_in, k_in, e_in = refs[0:8], refs[8:16], refs[16:19]
    row_in, col_in = refs[19:23], refs[23:27]
    q_out, k_out, inv_out = refs[27:31], refs[31:35], refs[35]
    q_s, k_s, e_s, wq, wk, out_s, inv, sems, out_sems = refs[36:45]
    loads = []
    for m in range(4):
        for i in range(3):
            rows = pl.ds(m * 256, 256)
            loads.append((e_in[i].at[rows], e_s.at[i, rows]))
    loads += [(ref, k_s.at[pl.ds(s * 256, 256)]) for s, ref in enumerate(k_in)]
    loads += [(ref, q_s.at[pl.ds(s * 256, 256)]) for s, ref in enumerate(q_in)]
    loads = [pltpu.make_async_copy(s, d, sems.at[i]) for i, (s, d) in enumerate(loads)]
    for load in loads:
        load.start()
    for at, ins in ((0, row_in), (16, col_in)):
        for rel in range(2):
            for slot in range(8):
                total = ins[0][rel * 8 + slot : rel * 8 + slot + 1, :]
                for step in (1, 2, 3):
                    src = rel * 8 + (slot - 2 * step) % 8
                    total = total + ins[step][src : src + 1, :]
                dst = at + rel * 8 + slot
                inv[dst : dst + 1, :] = 1.0 / total
    inv_out[0:1, :] = inv[0:1, :]
    inv_out[1:2, :] = inv[16:17, :]
    inv_out[2:8, :] = jnp.zeros((6, DOCS), F32)
    stores = []

    def put(i, ref, grad):
        out_s[i] = grad.astype(BF)
        stores.append(pltpu.make_async_copy(out_s.at[i], ref, out_sems.at[i]))
        stores[-1].start()

    for m in range(4):
        for load in loads[3 * m : 3 * m + 3]:
            load.wait()
        for a in (2 * m, 2 * m + 1):
            rows = slice(a * DOCS, (a + 1) * DOCS)
            far = slice((8 + a) * DOCS, (9 + a) * DOCS)
            col_own = jnp.broadcast_to(inv[a : a + 1, :], (DOCS, DOCS)).T
            col_oth = jnp.broadcast_to(inv[8 + a : 9 + a, :], (DOCS, DOCS)).T
            for b in range(8):
                near_key = inv[16 + b : 17 + b, :]
                far_key = inv[24 + b : 25 + b, :]
                keys = slice(b * DOCS, (b + 1) * DOCS)
                keys_far = slice((8 + b) * DOCS, (9 + b) * DOCS)
                w1 = (e_s[0, rows, keys].astype(F32) * (col_own + near_key)).astype(BF)
                w2 = (e_s[1, rows, keys].astype(F32) * (col_own + far_key)).astype(BF)
                w3 = (e_s[2, rows, keys].astype(F32) * (col_oth + near_key)).astype(BF)
                wq[rows, keys] = w1
                wq[rows, keys_far] = w2
                wk[rows, keys] = w1
                wk[far, keys] = w3
    for load in loads[12:20]:
        load.wait()
    for m in range(4):
        put(m, q_out[m], dot(wq[m * 256 : (m + 1) * 256, :], k_s[...]) * TAU_INV)
    for load in loads[20:]:
        load.wait()
    for m in range(4):
        put(4 + m, k_out[m], t_dot(wk[:, m * 256 : (m + 1) * 256], q_s[...]) * TAU_INV)
    for store in stores:
        store.wait()


def grads(q_in, k_in, e_in, row_in, col_in):
    return pl.pallas_call(
        grads_body,
        in_specs=[ANY] * 19 + [VMEM] * 8,
        out_specs=[ANY] * 8 + [VMEM],
        out_shape=[sds((256, EMB), BF)] * 8 + [sds((8, DOCS), F32)],
        scratch_shapes=[
            pltpu.VMEM((16 * DOCS, EMB), BF),
            pltpu.VMEM((16 * DOCS, EMB), BF),
            pltpu.VMEM((3, 8 * DOCS, 8 * DOCS), BF),
            pltpu.VMEM((8 * DOCS, 16 * DOCS), BF),
            pltpu.VMEM((16 * DOCS, 8 * DOCS), BF),
            pltpu.VMEM((8, 256, EMB), BF),
            pltpu.VMEM((32, DOCS), F32),
            pltpu.SemaphoreType.DMA((28,)),
            pltpu.SemaphoreType.DMA((8,)),
        ],
        compiler_params=params(),
    )(*q_in, *k_in, *e_in, *row_in, *col_in)


def half_block(which):
    return pl.BlockSpec((DOCS, EMB), lambda i: (which, 0))


def pass_body(*refs):
    for ins, out in ((refs[0:4], refs[8]), (refs[4:8], refs[9])):
        out[...] = sum(ref[...].astype(F32) for ref in ins).astype(BF)


def pass_on(query_in, key_in):
    return pl.pallas_call(
        pass_body,
        grid=(1,),
        in_specs=[half_block(1)] * 8,
        out_specs=[half_block(0)] * 2,
        out_shape=[sds((DOCS, EMB), BF)] * 2,
        compiler_params=params(),
    )(*query_in, *key_in)


def keep_body(*refs):
    q_parts, k_parts = refs[0:4], refs[4:8]
    q_unit, paired, q_perm, pos, inv, q_out, k_out = refs[8:15]
    hot = one_hot(pos[...])
    same = eye()
    pair = paired[...].astype(F32)
    score = jnp.sum(q_unit[...].astype(F32) * pair, axis=1, keepdims=True) * TAU_INV
    expo = jnp.exp(score)
    inv_r = jnp.sum(same * inv[0:1, :], axis=1, keepdims=True)
    inv_c = jnp.sum(hot * inv[1:2, :], axis=1, keepdims=True)
    weight = expo * inv_r + expo * inv_c - 2.0
    weight_k = jnp.sum(same * jnp.sum(hot * weight, axis=0, keepdims=True), axis=1, keepdims=True)
    for parts, w, pair_rows, out in (
        (q_parts, weight, pair, q_out),
        (k_parts, weight_k, q_perm[...].astype(F32), k_out),
    ):
        out[...] = sum(ref[...].astype(F32) for ref in parts) + (w * TAU_INV) * pair_rows


def keep(query_in, key_in, q_unit, paired, q_perm, pos, inv):
    return pl.pallas_call(
        keep_body,
        grid=(1,),
        in_specs=[half_block(0)] * 11 + [VMEM] * 2,
        out_specs=[half_block(0)] * 2,
        out_shape=[sds((DOCS, EMB), F32)] * 2,
        compiler_params=params(),
    )(*query_in, *key_in, q_unit, paired, q_perm, pos, inv)


def back_body(q_keep, q_got, k_keep, k_got, q_raw, k_raw, out):
    for kept, got, raw, start in ((q_keep, q_got, q_raw, 0), (k_keep, k_got, k_raw, DOCS)):
        grad = kept[...] + got[...].astype(F32)
        exact, scale = unit_of(raw[...])
        inner = jnp.sum(exact * grad, axis=1, keepdims=True)
        out[start : start + DOCS, :] = (scale * (grad - exact * inner)).astype(BF)


def back(*args):
    return pl.pallas_call(
        back_body,
        in_specs=[VMEM] * 6,
        out_specs=VMEM,
        out_shape=sds((2 * DOCS, EMB), BF),
        compiler_params=params(),
    )(*args)


def contract_body(*refs):
    b_in, h_in, where, out = refs[0:8], refs[8], refs[9], refs[10]
    h_s, b_s, sems = refs[11:14]
    loads = []
    for i in range(8):
        step, far = i % 4, i // 4
        source = ((where[2] - step) & 3) * 2 + (where[3] ^ far)
        loads.append((b_in[i], b_s.at[pl.ds(i * 256, 256)]))
        loads.append((h_in.at[source], h_s.at[:, pl.ds(i * 256, 256)]))
    loads = [pltpu.make_async_copy(s, d, sems.at[i]) for i, (s, d) in enumerate(loads)]
    for load in loads:
        load.start()
    for load in loads[:8]:
        load.wait()
    near = dot(h_s[:, :1024], b_s[:1024, :])
    for load in loads[8:]:
        load.wait()
    out[...] = (near + dot(h_s[:, 1024:], b_s[1024:, :])).astype(BF)


def contract(b_in, h_in, where):
    return pl.pallas_call(
        contract_body,
        in_specs=[ANY] * 9 + [SMEM],
        out_specs=VMEM,
        out_shape=sds((512, EMB), BF),
        scratch_shapes=[
            pltpu.VMEM((512, 2048), BF),
            pltpu.VMEM((2048, EMB), BF),
            pltpu.SemaphoreType.DMA((16,)),
        ],
        compiler_params=params(),
    )(*b_in, h_in, where)


def flip_slots(value):
    return value[:, ::-1]


def to_owners(parts, move):
    return [parts[0]] + [move(parts[(4 - step) % 4], step, 0) for step in (1, 2, 3)]


def local(hid_query, hid_key, projection, tile_rows, tile_cols, tile_count, positive):
    row_index = lax.axis_index("row")
    col_index = lax.axis_index("col")
    core_index = lax.axis_index("dp")
    x, z_hi = row_index // 2, row_index % 2
    y, z_lo = col_index // 2, col_index % 2
    where = jnp.stack([x, y, z_hi * 2 + z_lo, core_index]).astype(jnp.int32)

    q_unit, k_unit, q_raw, k_raw = project(hid_query, hid_key, projection)
    k_flip = move_key(k_unit, 0, 1)
    q_flip = move_query(q_unit, 0, 1)

    pos = (positive - ((row_index * 8 + col_index) * 2 + core_index) * DOCS).reshape(DOCS, 1)
    paired, q_perm, pos_rows = pair_up(q_unit, k_unit, pos)
    turned = jnp.concatenate([hid_query, hid_key], axis=0).T.reshape(4, 2, 4, 2, 2, 32, 256)
    turned = turned.transpose(1, 3, 4, 0, 2, 5, 6).reshape(4096, 256)
    entry_rows = tile_rows[0, 0]
    entry_cols = tile_cols[0, 0]
    used = jnp.arange(entry_rows.shape[0], dtype=jnp.int32) < tile_count[0, 0]
    slot_rows = ((y - entry_rows // 2) % 4) * 2 + (z_lo ^ (entry_rows % 2))
    slot_cols = ((x - entry_cols // 2) % 4) * 2 + (z_hi ^ (entry_cols % 2))
    eight = jnp.arange(8, dtype=jnp.int32)
    hit = (
        (slot_rows[:, None, None] == eight[None, :, None])
        & (slot_cols[:, None, None] == eight[None, None, :])
        & used[:, None, None]
    )
    mask = jnp.any(hit, axis=0).astype(F32)

    k_flip, q_flip, pos, paired, q_perm, pos_rows, turned, mask = lax.optimization_barrier(
        (k_flip, q_flip, pos, paired, q_perm, pos_rows, turned, mask)
    )
    k_pair = jnp.concatenate([k_unit, k_flip], axis=0)
    q_pair = jnp.concatenate([q_unit, q_flip], axis=0)
    h_all = lax.all_to_all(
        turned, ("row", "col", "dp"), 0, 0, tiled=True, axis_index_groups=Z_GROUPS
    ).reshape(8, 512, 256)
    k_own = [k_pair] + [move_key(k_pair, step, 0) for step in (1, 2, 3)]
    q_own = [q_pair] + [move_query(q_pair, step, 0) for step in (1, 2, 3)]
    k_oth = [swap(one) for one in k_own]
    q_oth = [swap(one) for one in q_own]
    mask, h_all = lax.optimization_barrier((mask, h_all))

    e_own, e_oth, sums = scores(q_own, k_own + k_oth, mask, pos_rows)
    far = swap(sums)
    e_rcv = swap(e_oth)
    row_part = jnp.concatenate([sums[:8], far[:8]], axis=0).reshape(8, 2, DOCS)
    col_part = sums[8:] + jnp.concatenate([far[16:], far[8:16]], axis=0)
    col_part = col_part.reshape(8, 2, DOCS)
    row_part = row_part + flip_slots(move_query(row_part, 0, 1))
    col_part = col_part + flip_slots(move_key(col_part, 0, 1))
    row_part = row_part.reshape(16, DOCS)
    col_part = col_part.reshape(16, DOCS)
    row_got = [row_part] + [move_query(row_part, step, 0) for step in (1, 2, 3)]
    col_got = [col_part] + [move_key(col_part, step, 0) for step in (1, 2, 3)]

    parts = grads(q_own + q_oth, k_own + k_oth, [e_own, e_oth, e_rcv], row_got, col_got)
    inv = parts[8]
    query_in = to_owners(parts[:4], move_query)
    key_in = to_owners(parts[4:8], move_key)
    q_send, k_send = pass_on(query_in, key_in)
    q_got = move_query(q_send, 0, 1)
    k_got = move_key(k_send, 0, 1)
    q_keep, k_keep = keep(query_in, key_in, q_unit, paired, q_perm, pos, inv)
    b_own = back(q_keep, q_got, k_keep, k_got, q_raw, k_raw)
    b_near = [b_own] + [move_z(b_own, step) for step in (1, 2, 3)]
    out = contract(b_near + [swap(one) for one in b_near], h_all, where)
    out = lax.all_to_all(out, ("row", "col"), 0, 0, tiled=True, axis_index_groups=XY_GROUPS)
    return jnp.sum(out.reshape(16, 32, EMB).astype(F32), axis=0)


def solution(mesh):
    return jax.shard_map(
        local,
        mesh=mesh,
        in_specs=(
            P(("row", "col", "dp"), None),
            P(("row", "col", "dp"), None),
            P(),
            P("row", "col", None),
            P("row", "col", None),
            P("row", "col"),
            P(("row", "col", "dp")),
        ),
        out_specs=P(("row", "col", "dp"), None),
        check_vma=False,
    )
```

time: 1420 us -> 233 us (0.16)
  waiting for transfers between devices: 941 us -> 89.1 us
  matrix products: 228 us -> 0 us
  local copies, waits for them, and re-layouts: 92.2 us -> 10.9 us
  loops' own time: 61.8 us -> 0 us
  starting transfers between devices: 0.17 us -> 52.8 us
  Pallas kernels: 0 us -> 51.7 us
  blocking collectives: 61.9 us -> 23.4 us
    reduce_scatter x3 -> x0, waiting for transfers between devices: 855 us -> none  [the longest x1 668 us: local(): lax.psum_scatter(contract_docs(hid_query, query_back) + contract_docs(hid...]
    dot_general x100 -> x0, matrix products: 228 us -> none  [the longest x26 76.9 us: contract_docs(): lax.dot_general(left, right, (((0,), (0,)), ((), ())), preferred_element_...]
    ppermute x0 -> x41, waiting for transfers between devices: none -> 89.1 us  [the longest x12 38.1 us: move_key(): return lax.ppermute(value, 'row', ring_pair(step, flip))]
    all_gather x2 -> x0, waiting for transfers between devices: 86.2 us -> none  [the longest x1 48.4 us: local(): key_block = lax.all_gather(key_unit, ('row', 'dp'), axis=0, tiled=True)]
    dynamic_slice x145 -> x0, local copies, waits for them, and re-layouts: 62.6 us -> none  [the longest x48 29.5 us: tile_at(): col_start = cell_cols[entry] * TILE]
    psum x2 -> x0, blocking collectives: 61.9 us -> none  [the longest x1 33.7 us: local(): col_log = jnp.log(lax.psum(col_sum, ('row', 'dp')))]
    another operation x2 -> x0, loops' own time: 61.8 us -> none  [the longest x1 33.9 us: local(): lax.fori_loop(0, my_tiles, first_pass, (row_sum, col_sum))]
    pallas_call x0 -> x8, Pallas kernels: none -> 51.7 us  [the longest x1 15.6 us: grads(): pl.pallas_call(grads_body, in_specs=[ANY] * 19 + [VMEM] * 8, out_specs=[A...]
  transfers between devices with their start and end apart: 5 -> 42, of which waited for: 5 -> 19; matrix products, arithmetic and copies ran while one was open for 1% -> 4% of each run, Pallas kernels for 0% -> 2%
where the time goes in v1:
time: 233 us; the launch traced here: 232 us
  waiting for transfers between devices  89.1 us (38%)
  starting transfers between devices  52.8 us (23%)
  Pallas kernels  51.7 us (22%)
  blocking collectives  23.4 us (10%)
  local copies, waits for them, and re-layouts  10.9 us (5%)
  other arithmetic  3.23 us (1%)
    ppermute x12, waiting for transfers between devices, move_key(): return lax.ppermute(value, 'row', ring_pair(step, flip))  38.1 us
    ppermute x12, waiting for transfers between devices, move_query(): return lax.ppermute(value, 'col', ring_pair(step, flip))  30.7 us
    all_to_all x1, blocking collectives, local(): lax.all_to_all(out, ('row', 'col'), 0, 0, tiled=True, axis_index_groups=X...  23.4 us
    ppermute x12, starting transfers between devices, move_key(): return lax.ppermute(value, 'row', ring_pair(step, flip))  21.7 us
    ppermute x12, starting transfers between devices, move_query(): return lax.ppermute(value, 'col', ring_pair(step, flip))  21.2 us
    pallas_call x1, Pallas kernels, grads(): pl.pallas_call(grads_body, in_specs=[ANY] * 19 + [VMEM] * 8, out_specs=[A...  15.6 us
    ppermute x3, waiting for transfers between devices, move_z(): return lax.ppermute(value, ('row', 'col'), pairs)  13.8 us
    pallas_call x1, Pallas kernels, scores(): pl.pallas_call(scores_body, in_specs=[ANY] * 12 + [SMEM, VMEM], out_specs...  11.4 us
  transfers between devices with their start and end apart: 42, of which 19 were waited for; matrix products, arithmetic and copies ran while one was open for 4% of the time, Pallas kernels for 2%

profile of v1, /device:TPU:0, one launch (start us, length us, event | category | flops | bytes accessed | tf_op | source)
XLA Modules:
  0.0 232.3 jit_solution(1973704751179255370)
XLA Ops:
  0.0 7.5 %shard_map.73 = (bf16[128,1024]{1,0:T(8,128)(2,1)}, bf16[128,1024]{1,0:T(8,128)(2,1)}, bf16[128,1024]{1,0:T(8,128)(2,1)}, bf16[128,1024]{1,0:T(8,128)(2,1)}) custom-call(bf16[128,4096]{1,0:T(8,128)(2,1)} %hq.1, bf16[128,4096]{1,0:T(8,128)(2,1)} %hk.1, bf16[4096,1024]{1,0:T(8,128)(2,1)} %proj.1), custom_call_target="tpu_custom_call" | custom-call | tf_op jit(solution)/shard_map/pallas_call | solution.py:112
  7.5 2.0 collective-permute-start.1
  9.5 3.6 %collective-permute-start = (bf16[128,1024]{1,0:T(8,128)(2,1)}, bf16[128,1024]{1,0:T(8,128)(2,1)}, u32[]{:S(2)}, u32[]{:S(2)}) collective-permute-start(bf16[128,1024]{1,0:T(8,128)(2,1)} %get-tuple-element.39.k_unit), channel_id=1, source_target_pairs={{0,16},{16,0},{32,48},{48,32},{64,80},{80,64},{96,112},{112,96},{1... | collective-permute-start | bytes 786440 | tf_op jit(solution)/shard_map/ppermute | solution.py:28
  16.8 2.1 shard_map.74
  20.6 4.4 %collective-permute-done = bf16[128,1024]{1,0:T(8,128)(2,1)} collective-permute-done((bf16[128,1024]{1,0:T(8,128)(2,1)}, bf16[128,1024]{1,0:T(8,128)(2,1)}, u32[]{:S(2)}, u32[]{:S(2)}) %collective-permute-start) | collective-permute-done | bytes 262176 | tf_op jit(solution)/shard_map/ppermute | solution.py:28
  25.0 3.7 %all-to-all-start = ((bf16[8,512,256]{2,1,0:T(8,128)(2,1)}), bf16[8,512,256]{2,1,0:T(8,128)(2,1)S(1)}, u32[]{:S(2)}, u32[]{:S(2)}) async-start(bf16[8,512,256]{2,1,0:T(8,128)(2,1)} %bitcast.8), calls=%async_computation | async-start | bytes 4194304 | tf_op jit(solution)/shard_map/all_to_all | solution.py:472
  31.4 2.7 %collective-permute-start.10 = (bf16[256,1024]{1,0:T(8,128)(2,1)S(1)}, bf16[256,1024]{1,0:T(8,128)(2,1)}, u32[]{:S(2)}, u32[]{:S(2)}) collective-permute-start(bf16[256,1024]{1,0:T(8,128)(2,1)S(1)} %constant_dynamic-update-slice_fusion.2.refs_4_.refs_8_), channel_id=1, source_target_pairs={{0,64},{16,80},{32,96},{48,112},{64,0},{80,16},{96,32},{112,48},{1... | collective-permute-start | bytes 1572872 | tf_op jit(solution)/shard_map/ppermute | solution.py:28
  38.2 7.2 %collective-permute-done.9.refs_5_.refs_9_ = bf16[256,1024]{1,0:T(8,128)(2,1)} collective-permute-done((bf16[256,1024]{1,0:T(8,128)(2,1)S(1)}, bf16[256,1024]{1,0:T(8,128)(2,1)}, u32[]{:S(2)}, u32[]{:S(2)}) %collective-permute-start.9) | collective-permute-done | bytes 524320 | tf_op jit(solution)/shard_map/ppermute | solution.py:28
  45.4 3.2 %collective-permute-start.3 = (bf16[256,1024]{1,0:T(8,128)(2,1)S(1)}, bf16[256,1024]{1,0:T(8,128)(2,1)}, u32[]{:S(2)}, u32[]{:S(2)}) collective-permute-start(bf16[256,1024]{1,0:T(8,128)(2,1)S(1)} %constant_dynamic-update-slice_fusion.refs_0_), channel_id=1, source_target_pairs={{0,8},{2,10},{4,12},{6,14},{8,0},{10,2},{12,4},{14,6},{1,9},{3,11}... | collective-permute-start | bytes 1572872 | tf_op jit(solution)/shard_map/ppermute | solution.py:24
  48.6 9.0 %collective-permute-done.10.refs_6_.refs_10_ = bf16[256,1024]{1,0:T(8,128)(2,1)} collective-permute-done((bf16[256,1024]{1,0:T(8,128)(2,1)S(1)}, bf16[256,1024]{1,0:T(8,128)(2,1)}, u32[]{:S(2)}, u32[]{:S(2)}) %collective-permute-start.10) | collective-permute-done | bytes 524320 | tf_op jit(solution)/shard_map/ppermute | solution.py:28
  57.7 3.0 %collective-permute-start.4 = (bf16[256,1024]{1,0:T(8,128)(2,1)S(1)}, bf16[256,1024]{1,0:T(8,128)(2,1)}, u32[]{:S(2)}, u32[]{:S(2)}) collective-permute-start(bf16[256,1024]{1,0:T(8,128)(2,1)S(1)} %constant_dynamic-update-slice_fusion.refs_0_), channel_id=1, source_target_pairs={{0,12},{2,14},{4,0},{6,2},{8,4},{10,6},{12,8},{14,10},{1,13},{3,15... | collective-permute-start | bytes 1572872 | tf_op jit(solution)/shard_map/ppermute | solution.py:24
  62.0 2.7 %collective-permute-done.3.refs_2_ = bf16[256,1024]{1,0:T(8,128)(2,1)} collective-permute-done((bf16[256,1024]{1,0:T(8,128)(2,1)S(1)}, bf16[256,1024]{1,0:T(8,128)(2,1)}, u32[]{:S(2)}, u32[]{:S(2)}) %collective-permute-start.3) | collective-permute-done | bytes 524320 | tf_op jit(solution)/shard_map/ppermute | solution.py:24
  64.8 7.2 %collective-permute-done.4.refs_3_ = bf16[256,1024]{1,0:T(8,128)(2,1)} collective-permute-done((bf16[256,1024]{1,0:T(8,128)(2,1)S(1)}, bf16[256,1024]{1,0:T(8,128)(2,1)}, u32[]{:S(2)}, u32[]{:S(2)}) %collective-permute-start.4) | collective-permute-done | bytes 524320 | tf_op jit(solution)/shard_map/ppermute | solution.py:24
  72.1 11.4 %shard_map.75 = (bf16[1024,1024]{1,0:T(8,128)(2,1)}, bf16[1024,1024]{1,0:T(8,128)(2,1)}, f32[24,128]{1,0:T(8,128)}) custom-call(bf16[256,1024]{1,0:T(8,128)(2,1)} %copy-done.3, bf16[256,1024]{1,0:T(8,128)(2,1)} %collective-permute-done.2.refs_1_, bf16[256,1024]{1,0:T(8,128)(2,1)} %collective-permute-done.3.refs_2_, ...), custom_call_target="tpu_custom_call" | custom-call | tf_op jit(solution)/shard_map/pallas_call | solution.py:219
  85.3 4.1 %collective-permute-done.17 = f32[24,128]{1,0:T(8,128)S(1)} collective-permute-done((f32[24,128]{1,0:T(8,128)}, f32[24,128]{1,0:T(8,128)S(1)}, u32[]{:S(2)}, u32[]{:S(2)}) %collective-permute-start.17) | collective-permute-done | bytes 12320 | tf_op jit(solution)/shard_map/ppermute | solution.py:53
  90.3 3.0 %collective-permute-start.22 = (f32[8,2,128]{2,1,0:T(2,128)S(1)}, f32[8,2,128]{2,1,0:T(2,128)S(1)}, u32[]{:S(2)}, u32[]{:S(2)}) collective-permute-start(f32[8,2,128]{2,1,0:T(2,128)S(1)} %bitcast.56), channel_id=1, source_target_pairs={{0,16},{16,0},{32,48},{48,32},{64,80},{80,64},{96,112},{112,96},{1... | collective-permute-start | bytes 24584 | tf_op jit(solution)/shard_map/ppermute | solution.py:28
  93.3 2.2 collective-permute-done.22
  99.2 1.8 collective-permute-start.24
  103.5 3.1 %collective-permute-start.20 = (f32[16,128]{1,0:T(8,128)S(1)}, f32[16,128]{1,0:T(8,128)S(1)}, u32[]{:S(2)}, u32[]{:S(2)}) collective-permute-start(f32[16,128]{1,0:T(8,128)S(1)} %bitcast.53), channel_id=1, source_target_pairs={{0,8},{2,10},{4,12},{6,14},{8,0},{10,2},{12,4},{14,6},{1,9},{3,11}... | collective-permute-start | bytes 24584 | tf_op jit(solution)/shard_map/ppermute | solution.py:24
  111.6 15.6 %shard_map.76 = (bf16[256,1024]{1,0:T(8,128)(2,1)}, bf16[256,1024]{1,0:T(8,128)(2,1)}, bf16[256,1024]{1,0:T(8,128)(2,1)}, bf16[256,1024]{1,0:T(8,128)(2,1)}, bf1...) custom-call(bf16[256,1024]{1,0:T(8,128)(2,1)} %copy-done.3, ...), custom_call_target="tpu_custom_call" | custom-call | tf_op jit(solution)/shard_map/pallas_call | solution.py:307
  127.3 3.8 %collective-permute-start.27 = (bf16[256,1024]{1,0:T(8,128)(2,1)}, bf16[256,1024]{1,0:T(8,128)(2,1)S(1)}, u32[]{:S(2)}, u32[]{:S(2)}) collective-permute-start(bf16[256,1024]{1,0:T(8,128)(2,1)} %get-tuple-element.54), channel_id=1, source_target_pairs={{0,8},{2,10},{4,12},{6,14},{8,0},{10,2},{12,4},{14,6},{1,9},{3,11}... | collective-permute-start | bytes 1572872 | tf_op jit(solution)/shard_map/ppermute | solution.py:24
  134.6 15.9 %collective-permute-done.26.refs_1_ = bf16[256,1024]{1,0:T(8,128)(2,1)S(1)} collective-permute-done((bf16[256,1024]{1,0:T(8,128)(2,1)}, bf16[256,1024]{1,0:T(8,128)(2,1)S(1)}, u32[]{:S(2)}, u32[]{:S(2)}) %collective-permute-start.26) | collective-permute-done | bytes 524320 | tf_op jit(solution)/shard_map/ppermute | solution.py:24
  151.1 2.7 %collective-permute-done.29.refs_5_ = bf16[256,1024]{1,0:T(8,128)(2,1)S(1)} collective-permute-done((bf16[256,1024]{1,0:T(8,128)(2,1)}, bf16[256,1024]{1,0:T(8,128)(2,1)S(1)}, u32[]{:S(2)}, u32[]{:S(2)}) %collective-permute-start.29) | collective-permute-done | bytes 524320 | tf_op jit(solution)/shard_map/ppermute | solution.py:28
  153.7 6.1 %collective-permute-done.31.refs_7_ = bf16[256,1024]{1,0:T(8,128)(2,1)S(1)} collective-permute-done((bf16[256,1024]{1,0:T(8,128)(2,1)}, bf16[256,1024]{1,0:T(8,128)(2,1)S(1)}, u32[]{:S(2)}, u32[]{:S(2)}) %collective-permute-start.31) | collective-permute-done | bytes 524320 | tf_op jit(solution)/shard_map/ppermute | solution.py:28
  160.6 2.5 %shard_map.78 = (bf16[128,1024]{1,0:T(8,128)(2,1)}, bf16[128,1024]{1,0:T(8,128)(2,1)}) custom-call(bf16[256,1024]{1,0:T(8,128)(2,1)} %get-tuple-element.52.refs_0_, bf16[256,1024]{1,0:T(8,128)(2,1)} %copy-done.8, bf16[256,1024]{1,0:T(8,128)(2,1)} %copy-done.9, bf16[256,1024]{1,0:T(8,128)(2,1)} %copy-done.10, bf16[256,1024]{1,0:T(8,128)(2,1)} %get-tuple-element.56.refs_4_, ...), custom_call_target="tpu_custom_call" | custom-call | tf_op jit(solution)/shard_map/pallas_call | solution.py:337
  163.4 2.7 %collective-permute-start.33 = (bf16[128,1024]{1,0:T(8,128)(2,1)}, bf16[128,1024]{1,0:T(8,128)(2,1)S(1)}, u32[]{:S(2)}, u32[]{:S(2)}) collective-permute-start(bf16[128,1024]{1,0:T(8,128)(2,1)} %get-tuple-element.67), channel_id=1, source_target_pairs={{0,16},{16,0},{32,48},{48,32},{64,80},{80,64},{96,112},{112,96},{1... | collective-permute-start | bytes 786440 | tf_op jit(solution)/shard_map/ppermute | solution.py:28
  166.9 3.0 %shard_map.77 = (f32[128,1024]{1,0:T(8,128)}, f32[128,1024]{1,0:T(8,128)}) custom-call(bf16[256,1024]{1,0:T(8,128)(2,1)} %get-tuple-element.52.refs_0_, bf16[256,1024]{1,0:T(8,128)(2,1)} %copy-done.8, bf16[256,1024]{1,0:T(8,128)(2,1)} %copy-done.9, bf16[256,1024]{1,0:T(8,128)(2,1)} %copy-done.10, bf16[256,1024]{1,0:T(8,128)(2,1)} %get-tuple-element.56.refs_4_, ...), custom_call_target="tpu_custom_call" | custom-call | tf_op jit(solution)/shard_map/pallas_call | solution.py:367
  169.9 6.5 %collective-permute-done.33.k_got = bf16[128,1024]{1,0:T(8,128)(2,1)S(1)} collective-permute-done((bf16[128,1024]{1,0:T(8,128)(2,1)}, bf16[128,1024]{1,0:T(8,128)(2,1)S(1)}, u32[]{:S(2)}, u32[]{:S(2)}) %collective-permute-start.33) | collective-permute-done | bytes 262176 | tf_op jit(solution)/shard_map/ppermute | solution.py:28
  177.1 2.7 %shard_map.79.refs_0_ = bf16[256,1024]{1,0:T(8,128)(2,1)} custom-call(f32[128,1024]{1,0:T(8,128)} %get-tuple-element.64.q_keep, bf16[128,1024]{1,0:T(8,128)(2,1)} %copy-done.23, f32[128,1024]{1,0:T(8,128)} %get-tuple-element.66.k_keep, bf16[128,1024]{1,0:T(8,128)(2,1)} %copy-done.24, bf16[128,1024]{1,0:T(8,128)(2,1)} %get-tuple-element.68.q_raw, ...), custom_call_target="tpu_custom_call" | custom-call | tf_op jit(solution)/shard_map/pallas_call | solution.py:386
  183.1 13.8 %collective-permute-done.34.refs_1_ = bf16[256,1024]{1,0:T(8,128)(2,1)S(1)} collective-permute-done((bf16[256,1024]{1,0:T(8,128)(2,1)}, bf16[256,1024]{1,0:T(8,128)(2,1)S(1)}, u32[]{:S(2)}, u32[]{:S(2)}) %collective-permute-start.34) | collective-permute-done | bytes 524320 | tf_op jit(solution)/shard_map/ppermute | solution.py:37
  201.1 6.9 %shard_map.80 = bf16[512,1024]{1,0:T(8,128)(2,1)} custom-call(bf16[256,1024]{1,0:T(8,128)(2,1)} %shard_map.79.refs_0_, bf16[256,1024]{1,0:T(8,128)(2,1)} %copy-done.17, bf16[256,1024]{1,0:T(8,128)(2,1)} %copy-done.18, bf16[256,1024]{1,0:T(8,128)(2,1)} %copy-done.19, bf16[256,1024]{1,0:T(8,128)(2,1)} %copy-done.20, bf16[256,1024]{1,0:T(8,128)(2,1)} %copy-done.21, ...), custom_call_target="tpu_custom_call" | custom-call | tf_op jit(solution)/shard_map/pallas_call | solution.py:416
  208.0 23.4 %all_to_all.18 = bf16[16,32,1024]{2,1,0:T(8,128)(2,1)S(1)} all-to-all(bf16[16,32,1024]{2,1,0:T(8,128)(2,1)} %bitcast.47), channel_id=1, replica_groups={{0,4,8,12,32,36,40,44,64,68,72,76,96,100,104,108},{2,6,10,14,34,38,42,4..., dimensions={0} | all-to-all | bytes 2097152 | tf_op jit(solution)/shard_map/all_to_all | solution.py:505
  (162 shorter events, 41.4 us)
Async XLA Ops:
  7.5 13.1 %collective-permute-start.1 = (bf16[128,1024]{1,0:T(8,128)(2,1)}, bf16[128,1024]{1,0:T(8,128)(2,1)S(1)}, u32[]{:S(2)}, u32[]{:S(2)}) collective-permute-start(bf16[128,1024]{1,0:T(8,128)(2,1)} %get-tuple-element.38.q_unit.refs_8_), channel_id=1, source_target_pairs={{0,2},{2,0},{4,6},{6,4},{8,10},{10,8},{12,14},{14,12},{1,3},{3,1},... | collective-permute-start | bytes 786440 | tf_op jit(solution)/shard_map/ppermute | solution.py:24
  9.5 15.5 %collective-permute-start = (bf16[128,1024]{1,0:T(8,128)(2,1)}, bf16[128,1024]{1,0:T(8,128)(2,1)}, u32[]{:S(2)}, u32[]{:S(2)}) collective-permute-start(bf16[128,1024]{1,0:T(8,128)(2,1)} %get-tuple-element.39.k_unit), channel_id=1, source_target_pairs={{0,16},{16,0},{32,48},{48,32},{64,80},{80,64},{96,112},{112,96},{1... | collective-permute-start | bytes 786440 | tf_op jit(solution)/shard_map/ppermute | solution.py:28
  25.0 37.0 %all-to-all-start = ((bf16[8,512,256]{2,1,0:T(8,128)(2,1)}), bf16[8,512,256]{2,1,0:T(8,128)(2,1)S(1)}, u32[]{:S(2)}, u32[]{:S(2)}) async-start(bf16[8,512,256]{2,1,0:T(8,128)(2,1)} %bitcast.8), calls=%async_computation | async-start | bytes 4194304 | tf_op jit(solution)/shard_map/all_to_all | solution.py:472
  29.8 15.6 %collective-permute-start.9 = (bf16[256,1024]{1,0:T(8,128)(2,1)S(1)}, bf16[256,1024]{1,0:T(8,128)(2,1)}, u32[]{:S(2)}, u32[]{:S(2)}) collective-permute-start(bf16[256,1024]{1,0:T(8,128)(2,1)S(1)} %constant_dynamic-update-slice_fusion.2.refs_4_.refs_8_), channel_id=1, source_target_pairs={{0,32},{16,48},{32,64},{48,80},{64,96},{80,112},{96,0},{112,16},{1... | collective-permute-start | bytes 1572872 | tf_op jit(solution)/shard_map/ppermute | solution.py:28
  31.4 26.2 %collective-permute-start.10 = (bf16[256,1024]{1,0:T(8,128)(2,1)S(1)}, bf16[256,1024]{1,0:T(8,128)(2,1)}, u32[]{:S(2)}, u32[]{:S(2)}) collective-permute-start(bf16[256,1024]{1,0:T(8,128)(2,1)S(1)} %constant_dynamic-update-slice_fusion.2.refs_4_.refs_8_), channel_id=1, source_target_pairs={{0,64},{16,80},{32,96},{48,112},{64,0},{80,16},{96,32},{112,48},{1... | collective-permute-start | bytes 1572872 | tf_op jit(solution)/shard_map/ppermute | solution.py:28
  34.2 26.5 %collective-permute-start.11 = (bf16[256,1024]{1,0:T(8,128)(2,1)S(1)}, bf16[256,1024]{1,0:T(8,128)(2,1)}, u32[]{:S(2)}, u32[]{:S(2)}) collective-permute-start(bf16[256,1024]{1,0:T(8,128)(2,1)S(1)} %constant_dynamic-update-slice_fusion.2.refs_4_.refs_8_), channel_id=1, source_target_pairs={{0,96},{16,112},{32,0},{48,16},{64,32},{80,48},{96,64},{112,80},{1... | collective-permute-start | bytes 1572872 | tf_op jit(solution)/shard_map/ppermute | solution.py:28
  35.6 25.1 %collective-permute-start.12 = (bf16[256,1024]{1,0:T(8,128)(2,1)S(1)}, bf16[256,1024]{1,0:T(8,128)(2,1)S(1)}, u32[]{:S(2)}, u32[]{:S(2)}) collective-permute-start(bf16[256,1024]{1,0:T(8,128)(2,1)S(1)} %constant_dynamic-update-slice_fusion.2.refs_4_.refs_8_), channel_id=1, source_target_pairs={{0,1},{1,0},{2,3},{3,2},{4,5},{5,4},{6,7},{7,6},{8,9},{9,8},{10,11... | collective-permute-start | bytes 1572872 | tf_op jit(solution)/shard_map/ppermute | solution.py:53
  36.6 24.6 %collective-permute-start.2 = (bf16[256,1024]{1,0:T(8,128)(2,1)S(1)}, bf16[256,1024]{1,0:T(8,128)(2,1)}, u32[]{:S(2)}, u32[]{:S(2)}) collective-permute-start(bf16[256,1024]{1,0:T(8,128)(2,1)S(1)} %constant_dynamic-update-slice_fusion.refs_0_), channel_id=1, source_target_pairs={{0,4},{2,6},{4,8},{6,10},{8,12},{10,14},{12,0},{14,2},{1,5},{3,7},... | collective-permute-start | bytes 1572872 | tf_op jit(solution)/shard_map/ppermute | solution.py:24
  45.4 19.3 %collective-permute-start.3 = (bf16[256,1024]{1,0:T(8,128)(2,1)S(1)}, bf16[256,1024]{1,0:T(8,128)(2,1)}, u32[]{:S(2)}, u32[]{:S(2)}) collective-permute-start(bf16[256,1024]{1,0:T(8,128)(2,1)S(1)} %constant_dynamic-update-slice_fusion.refs_0_), channel_id=1, source_target_pairs={{0,8},{2,10},{4,12},{6,14},{8,0},{10,2},{12,4},{14,6},{1,9},{3,11}... | collective-permute-start | bytes 1572872 | tf_op jit(solution)/shard_map/ppermute | solution.py:24
  57.7 14.4 %collective-permute-start.4 = (bf16[256,1024]{1,0:T(8,128)(2,1)S(1)}, bf16[256,1024]{1,0:T(8,128)(2,1)}, u32[]{:S(2)}, u32[]{:S(2)}) collective-permute-start(bf16[256,1024]{1,0:T(8,128)(2,1)S(1)} %constant_dynamic-update-slice_fusion.refs_0_), channel_id=1, source_target_pairs={{0,12},{2,14},{4,0},{6,2},{8,4},{10,6},{12,8},{14,10},{1,13},{3,15... | collective-permute-start | bytes 1572872 | tf_op jit(solution)/shard_map/ppermute | solution.py:24
  60.7 11.3 %collective-permute-start.13 = (bf16[256,1024]{1,0:T(8,128)(2,1)}, bf16[256,1024]{1,0:T(8,128)(2,1)}, u32[]{:S(2)}, u32[]{:S(2)}) collective-permute-start(bf16[256,1024]{1,0:T(8,128)(2,1)} %collective-permute-done.9.refs_5_.refs_9_), channel_id=1, source_target_pairs={{0,1},{1,0},{2,3},{3,2},{4,5},{5,4},{6,7},{7,6},{8,9},{9,8},{10,11... | collective-permute-start | bytes 1572872 | tf_op jit(solution)/shard_map/ppermute | solution.py:53
  60.7 11.3 %collective-permute-start.14 = (bf16[256,1024]{1,0:T(8,128)(2,1)}, bf16[256,1024]{1,0:T(8,128)(2,1)}, u32[]{:S(2)}, u32[]{:S(2)}) collective-permute-start(bf16[256,1024]{1,0:T(8,128)(2,1)} %collective-permute-done.10.refs_6_.refs_10_), channel_id=1, source_target_pairs={{0,1},{1,0},{2,3},{3,2},{4,5},{5,4},{6,7},{7,6},{8,9},{9,8},{10,11... | collective-permute-start | bytes 1572872 | tf_op jit(solution)/shard_map/ppermute | solution.py:53
  61.5 10.5 %collective-permute-start.15 = (bf16[256,1024]{1,0:T(8,128)(2,1)}, bf16[256,1024]{1,0:T(8,128)(2,1)}, u32[]{:S(2)}, u32[]{:S(2)}) collective-permute-start(bf16[256,1024]{1,0:T(8,128)(2,1)} %collective-permute-done.11.refs_7_.refs_11_), channel_id=1, source_target_pairs={{0,1},{1,0},{2,3},{3,2},{4,5},{5,4},{6,7},{7,6},{8,9},{9,8},{10,11... | collective-permute-start | bytes 1572872 | tf_op jit(solution)/shard_map/ppermute | solution.py:53
  83.5 26.8 %collective-permute-start.16 = (bf16[1024,1024]{1,0:T(8,128)(2,1)}, bf16[1024,1024]{1,0:T(8,128)(2,1)S(1)}, u32[]{:S(2)}, u32[]{:S(2)}) collective-permute-start(bf16[1024,1024]{1,0:T(8,128)(2,1)} %get-tuple-element.50.refs_17_), channel_id=1, source_target_pairs={{0,1},{1,0},{2,3},{3,2},{4,5},{5,4},{6,7},{7,6},{8,9},{9,8},{10,11... | collective-permute-start | bytes 6291464 | tf_op jit(solution)/shard_map/ppermute | solution.py:53
  83.6 6.7 %collective-permute-start.5 = (bf16[256,1024]{1,0:T(8,128)(2,1)}, bf16[256,1024]{1,0:T(8,128)(2,1)S(1)}, u32[]{:S(2)}, u32[]{:S(2)}) collective-permute-start(bf16[256,1024]{1,0:T(8,128)(2,1)} %copy-done.3), channel_id=1, source_target_pairs={{0,1},{1,0},{2,3},{3,2},{4,5},{5,4},{6,7},{7,6},{8,9},{9,8},{10,11... | collective-permute-start | bytes 1572872 | tf_op jit(solution)/shard_map/ppermute | solution.py:53
  84.2 12.9 %collective-permute-start.6 = (bf16[256,1024]{1,0:T(8,128)(2,1)}, bf16[256,1024]{1,0:T(8,128)(2,1)S(1)}, u32[]{:S(2)}, u32[]{:S(2)}) collective-permute-start(bf16[256,1024]{1,0:T(8,128)(2,1)} %collective-permute-done.2.refs_1_), channel_id=1, source_target_pairs={{0,1},{1,0},{2,3},{3,2},{4,5},{5,4},{6,7},{7,6},{8,9},{9,8},{10,11... | collective-permute-start | bytes 1572872 | tf_op jit(solution)/shard_map/ppermute | solution.py:53
  84.6 16.5 %collective-permute-start.7 = (bf16[256,1024]{1,0:T(8,128)(2,1)}, bf16[256,1024]{1,0:T(8,128)(2,1)}, u32[]{:S(2)}, u32[]{:S(2)}) collective-permute-start(bf16[256,1024]{1,0:T(8,128)(2,1)} %collective-permute-done.3.refs_2_), channel_id=1, source_target_pairs={{0,1},{1,0},{2,3},{3,2},{4,5},{5,4},{6,7},{7,6},{8,9},{9,8},{10,11... | collective-permute-start | bytes 1572872 | tf_op jit(solution)/shard_map/ppermute | solution.py:53
  89.4 12.9 %collective-permute-start.8 = (bf16[256,1024]{1,0:T(8,128)(2,1)}, bf16[256,1024]{1,0:T(8,128)(2,1)}, u32[]{:S(2)}, u32[]{:S(2)}) collective-permute-start(bf16[256,1024]{1,0:T(8,128)(2,1)} %collective-permute-done.4.refs_3_), channel_id=1, source_target_pairs={{0,1},{1,0},{2,3},{3,2},{4,5},{5,4},{6,7},{7,6},{8,9},{9,8},{10,11... | collective-permute-start | bytes 1572872 | tf_op jit(solution)/shard_map/ppermute | solution.py:53
  99.2 7.4 %collective-permute-start.24 = (f32[16,128]{1,0:T(8,128)S(1)}, f32[16,128]{1,0:T(8,128)S(1)}, u32[]{:S(2)}, u32[]{:S(2)}) collective-permute-start(f32[16,128]{1,0:T(8,128)S(1)} %bitcast.49), channel_id=1, source_target_pairs={{0,64},{16,80},{32,96},{48,112},{64,0},{80,16},{96,32},{112,48},{1... | collective-permute-start | bytes 24584 | tf_op jit(solution)/shard_map/ppermute | solution.py:28
  101.1 6.7 %collective-permute-start.25 = (f32[16,128]{1,0:T(8,128)S(1)}, f32[16,128]{1,0:T(8,128)S(1)}, u32[]{:S(2)}, u32[]{:S(2)}) collective-permute-start(f32[16,128]{1,0:T(8,128)S(1)} %bitcast.50), channel_id=1, source_target_pairs={{0,96},{16,112},{32,0},{48,16},{64,32},{80,48},{96,64},{112,80},{1... | collective-permute-start | bytes 24584 | tf_op jit(solution)/shard_map/ppermute | solution.py:28
  127.2 23.2 %collective-permute-start.26 = (bf16[256,1024]{1,0:T(8,128)(2,1)}, bf16[256,1024]{1,0:T(8,128)(2,1)S(1)}, u32[]{:S(2)}, u32[]{:S(2)}) collective-permute-start(bf16[256,1024]{1,0:T(8,128)(2,1)} %get-tuple-element.53), channel_id=1, source_target_pairs={{0,4},{2,6},{4,8},{6,10},{8,12},{10,14},{12,0},{14,2},{1,5},{3,7},... | collective-permute-start | bytes 1572872 | tf_op jit(solution)/shard_map/ppermute | solution.py:24
  127.3 23.2 %collective-permute-start.27 = (bf16[256,1024]{1,0:T(8,128)(2,1)}, bf16[256,1024]{1,0:T(8,128)(2,1)S(1)}, u32[]{:S(2)}, u32[]{:S(2)}) collective-permute-start(bf16[256,1024]{1,0:T(8,128)(2,1)} %get-tuple-element.54), channel_id=1, source_target_pairs={{0,8},{2,10},{4,12},{6,14},{8,0},{10,2},{12,4},{14,6},{1,9},{3,11}... | collective-permute-start | bytes 1572872 | tf_op jit(solution)/shard_map/ppermute | solution.py:24
  131.1 19.9 %collective-permute-start.28 = (bf16[256,1024]{1,0:T(8,128)(2,1)}, bf16[256,1024]{1,0:T(8,128)(2,1)S(1)}, u32[]{:S(2)}, u32[]{:S(2)}) collective-permute-start(bf16[256,1024]{1,0:T(8,128)(2,1)} %get-tuple-element.55), channel_id=1, source_target_pairs={{0,12},{2,14},{4,0},{6,2},{8,4},{10,6},{12,8},{14,10},{1,13},{3,15... | collective-permute-start | bytes 1572872 | tf_op jit(solution)/shard_map/ppermute | solution.py:24
  131.4 22.3 %collective-permute-start.29 = (bf16[256,1024]{1,0:T(8,128)(2,1)}, bf16[256,1024]{1,0:T(8,128)(2,1)S(1)}, u32[]{:S(2)}, u32[]{:S(2)}) collective-permute-start(bf16[256,1024]{1,0:T(8,128)(2,1)} %get-tuple-element.57), channel_id=1, source_target_pairs={{0,32},{16,48},{32,64},{48,80},{64,96},{80,112},{96,0},{112,16},{1... | collective-permute-start | bytes 1572872 | tf_op jit(solution)/shard_map/ppermute | solution.py:28
  132.9 20.9 %collective-permute-start.30 = (bf16[256,1024]{1,0:T(8,128)(2,1)}, bf16[256,1024]{1,0:T(8,128)(2,1)S(1)}, u32[]{:S(2)}, u32[]{:S(2)}) collective-permute-start(bf16[256,1024]{1,0:T(8,128)(2,1)} %get-tuple-element.58), channel_id=1, source_target_pairs={{0,64},{16,80},{32,96},{48,112},{64,0},{80,16},{96,32},{112,48},{1... | collective-permute-start | bytes 1572872 | tf_op jit(solution)/shard_map/ppermute | solution.py:28
  150.4 9.4 %collective-permute-start.31 = (bf16[256,1024]{1,0:T(8,128)(2,1)}, bf16[256,1024]{1,0:T(8,128)(2,1)S(1)}, u32[]{:S(2)}, u32[]{:S(2)}) collective-permute-start(bf16[256,1024]{1,0:T(8,128)(2,1)} %get-tuple-element.59), channel_id=1, source_target_pairs={{0,96},{16,112},{32,0},{48,16},{64,32},{80,48},{96,64},{112,80},{1... | collective-permute-start | bytes 1572872 | tf_op jit(solution)/shard_map/ppermute | solution.py:28
  163.1 6.8 %collective-permute-start.32 = (bf16[128,1024]{1,0:T(8,128)(2,1)}, bf16[128,1024]{1,0:T(8,128)(2,1)S(1)}, u32[]{:S(2)}, u32[]{:S(2)}) collective-permute-start(bf16[128,1024]{1,0:T(8,128)(2,1)} %get-tuple-element.65), channel_id=1, source_target_pairs={{0,2},{2,0},{4,6},{6,4},{8,10},{10,8},{12,14},{14,12},{1,3},{3,1},... | collective-permute-start | bytes 786440 | tf_op jit(solution)/shard_map/ppermute | solution.py:24
  163.4 13.0 %collective-permute-start.33 = (bf16[128,1024]{1,0:T(8,128)(2,1)}, bf16[128,1024]{1,0:T(8,128)(2,1)S(1)}, u32[]{:S(2)}, u32[]{:S(2)}) collective-permute-start(bf16[128,1024]{1,0:T(8,128)(2,1)} %get-tuple-element.67), channel_id=1, source_target_pairs={{0,16},{16,0},{32,48},{48,32},{64,80},{80,64},{96,112},{112,96},{1... | collective-permute-start | bytes 786440 | tf_op jit(solution)/shard_map/ppermute | solution.py:28
  179.8 17.1 %collective-permute-start.34 = (bf16[256,1024]{1,0:T(8,128)(2,1)}, bf16[256,1024]{1,0:T(8,128)(2,1)S(1)}, u32[]{:S(2)}, u32[]{:S(2)}) collective-permute-start(bf16[256,1024]{1,0:T(8,128)(2,1)} %shard_map.79.refs_0_), channel_id=1, source_target_pairs={{0,2},{2,16},{4,6},{6,20},{8,10},{10,24},{12,14},{14,28},{16,18},{... | collective-permute-start | bytes 1572872 | tf_op jit(solution)/shard_map/ppermute | solution.py:37
  179.8 17.1 %collective-permute-start.35 = (bf16[256,1024]{1,0:T(8,128)(2,1)}, bf16[256,1024]{1,0:T(8,128)(2,1)S(1)}, u32[]{:S(2)}, u32[]{:S(2)}) collective-permute-start(bf16[256,1024]{1,0:T(8,128)(2,1)} %shard_map.79.refs_0_), channel_id=1, source_target_pairs={{0,16},{2,18},{4,20},{6,22},{8,24},{10,26},{12,28},{14,30},{16,0},... | collective-permute-start | bytes 1572872 | tf_op jit(solution)/shard_map/ppermute | solution.py:37
  181.2 16.2 %collective-permute-start.36 = (bf16[256,1024]{1,0:T(8,128)(2,1)}, bf16[256,1024]{1,0:T(8,128)(2,1)S(1)}, u32[]{:S(2)}, u32[]{:S(2)}) collective-permute-start(bf16[256,1024]{1,0:T(8,128)(2,1)} %shard_map.79.refs_0_), channel_id=1, source_target_pairs={{0,18},{2,0},{4,22},{6,4},{8,26},{10,8},{12,30},{14,12},{16,2},{18... | collective-permute-start | bytes 1572872 | tf_op jit(solution)/shard_map/ppermute | solution.py:37
  183.1 15.0 %collective-permute-start.37 = (bf16[256,1024]{1,0:T(8,128)(2,1)}, bf16[256,1024]{1,0:T(8,128)(2,1)S(1)}, u32[]{:S(2)}, u32[]{:S(2)}) collective-permute-start(bf16[256,1024]{1,0:T(8,128)(2,1)} %shard_map.79.refs_0_), channel_id=1, source_target_pairs={{0,1},{1,0},{2,3},{3,2},{4,5},{5,4},{6,7},{7,6},{8,9},{9,8},{10,11... | collective-permute-start | bytes 1572872 | tf_op jit(solution)/shard_map/ppermute | solution.py:53
  (47 other events, 319.5 us)
